TPU v7x, 32 devices: a whole 2x2x4 slice. The times are simulated.
32 devices in a mesh: real: 2 (over y), col: 8 (over z, x), row: 2 (over core).
Axes of the slice: x: 2, y: 2, z: 4, core: 2. Of those that a mesh axis runs over, the one named last changes fastest.
Arguments:
- theta: bfloat16 [512, 16384], P(('real', 'row'), 'col'), parts along dimension 0, may hold values from -6 to 6
- signs: int32 [32768], P(('real', 'col')), parts along dimension 0, may hold values from -1 to 1, as said below
- kept: int32 [1024], replicated, may hold values from 0 to 16383, as said below
Outputs:
- gram: float32 [4, 8, 16, 256], P(('real', 'row'), 'col'), parts along dimension 0
There are 2 independent parts, one for each index of `real`. A program takes and returns all parts, laid end to end along the dimension named above; an argument that names none is the same for every part. Nothing has to cross between parts.
Inputs may be any that keep to these rules, and one draw needn't show every extreme that they name: `signs`: each entry is -1 or 1. `kept`: 1024 distinct column indices.
All inputs are finite; a program needn't handle non-finite values.
Results may differ from a plain program's by a relative error of at most 0.0036.
Values may be sent and summed in bfloat16 or wider, within the bound.
A program may use at most 64 MiB of HBM per device.

v0:
```python
import jax
import jax.numpy as jnp
from jax import lax
from jax.sharding import PartitionSpec as P

SIDE = 128
KEEP = 1024


def hadamard(order, dtype):
    indices = jnp.arange(order, dtype=jnp.int32)
    common = indices[:, None] & indices[None, :]
    parity = jnp.zeros((order, order), jnp.int32)
    for position in range(order.bit_length() - 1):
        parity = parity ^ common >> position & 1
    return (1 - 2 * parity).astype(dtype)


def against(left, right):
    return jnp.dot(left, right.T, preferred_element_type=jnp.float32)


def two_factor(spread):
    height = spread.shape[0]
    flat = spread.reshape(height * SIDE, SIDE)
    inner = jnp.dot(flat, hadamard(SIDE, jnp.bfloat16), preferred_element_type=jnp.float32).reshape(
        height, SIDE, SIDE
    )
    outer = jnp.einsum(
        "rak,aj->rjk", inner, hadamard(SIDE, jnp.float32), precision=lax.Precision.HIGHEST
    )
    return outer.reshape(height, SIDE * SIDE)


def per_device(theta, signs, kept):
    scaled = theta * signs.astype(jnp.bfloat16)[None, :]
    spread = lax.all_to_all(scaled, "col", split_axis=0, concat_axis=1, tiled=True)
    transformed = two_factor(spread) / SIDE
    sketch = jnp.take(transformed, kept, axis=1).astype(jnp.bfloat16)
    own_rows = sketch.shape[0]
    half_rows = lax.all_gather(sketch, "col", axis=0, tiled=True)
    gram = against(sketch, lax.all_gather(half_rows, "row", axis=0, tiled=True))
    return (gram / KEEP).reshape(1, 1, own_rows, gram.shape[1])


def solution(mesh):
    return jax.shard_map(
        per_device,
        mesh=mesh,
        in_specs=(P(("real", "row"), "col"), P(("real", "col")), P()),
        out_specs=P(("real", "row"), "col", None, None),
        check_vma=False,
    )
```

profile of v0, /device:TPU:0, one launch (start us, length us, event | category | flops | bytes accessed | tf_op | source)
XLA Modules:
  0.0 69.4 jit_solution(3105334876577274971)
XLA Ops:
  0.0 0.7 %convert_element_type.13 = bf16[2048]{0:T(1024)(128)(2,1)S(1)} convert(s32[2048]{0:T(1024)} %param.4) | non-fusion elementwise | flops 2048 | bytes 12288 | tf_op jit(solution)/shard_map/convert_element_type | solution.py:36
  0.7 1.9 %broadcast_multiply_fusion = bf16[128,2048]{1,0:T(8,128)(2,1)} fusion(bf16[128,2048]{1,0:T(8,128)(2,1)} %param.3, bf16[2048]{0:T(1024)(128)(2,1)S(1)} %convert_element_type.13), kind=kLoop, calls=%fused_computation.6 | loop fusion | flops 262144 | bytes 1052672 | tf_op jit(solution)/shard_map/mul | solution.py:36
  2.6 7.3 %all-to-all-start = ((bf16[8,16,2048]{2,1,0:T(8,128)(2,1)}), bf16[8,16,2048]{2,1,0:T(8,128)(2,1)S(1)}, u32[]{:S(2)}, u32[]{:S(2)}) async-start(bf16[8,16,2048]{2,1,0:T(8,128)(2,1)} %bitcast.1), calls=%async_computation | async-start | bytes 1048576 | tf_op jit(solution)/shard_map/all_to_all | solution.py:37
  9.8 0.7 compare_and_fusion
  10.5 0.7 fusion.7
  11.2 13.1 %all-to-all-done = bf16[8,16,2048]{2,1,0:T(8,128)(2,1)S(1)} async-done(((bf16[8,16,2048]{2,1,0:T(8,128)(2,1)}), bf16[8,16,2048]{2,1,0:T(8,128)(2,1)S(1)}, u32[]{:S(2)}, u32[]{:S(2)}) %all-to-all-start) | async-done | bytes 524320 | tf_op jit(solution)/shard_map/all_to_all | solution.py:37
  24.3 0.3 copy.7
  24.6 0.2 dot_general.11
  24.8 0.3 fusion.4
  25.2 1.1 %fusion = bf16[16,128,128]{2,1,0:T(8,128)(2,1)S(1)} fusion(f32[16,128,128]{2,1,0:T(8,128)S(1)} %fusion.4), kind=kOutput, calls=%fused_computation.2 | convolution fusion | flops 403570688 | bytes 1572864 | tf_op jit(solution)/shard_map/rak,aj->rjk/dot_general | solution.py:29
  26.3 3.2 %copy.13 = bf16[16,128,128]{0,2,1:T(8,128)(2,1)} copy(bf16[16,128,128]{2,1,0:T(8,128)(2,1)S(1)} %fusion) | data formatting | bytes 1048576 | tf_op jit(solution)/shard_map/div | solution.py:38
  29.4 5.6 %gather_fusion = bf16[1024,16]{1,0:T(8,128)(2,1)S(1)} fusion(bf16[16,16384]{0,1:T(8,128)(2,1)} %bitcast.18, s32[1024]{0:T(1024)S(1)} %fusion.7), kind=kCustom, calls=%fused_computation | custom fusion | bytes 69632 | tf_op jit(solution)/shard_map/jit(_take)/gather | solution.py:39
  35.0 0.2 fusion.22
  35.3 0.1 copy.10
  35.4 30.7 %all_gather.6 = bf16[128,1024]{1,0:T(8,128)(2,1)S(1)} all-gather(bf16[16,1024]{1,0:T(8,128)(2,1)S(1)} %copy.10), channel_id=1, replica_groups=mesh['real'=2,'col'=8,'row'=2] {'col'}, dimensions={0}, use_global_device_ids=true | all-gather | bytes 294912 | tf_op jit(solution)/shard_map/all_gather | solution.py:41
  66.1 2.2 %all_gather.7 = bf16[256,1024]{1,0:T(8,128)(2,1)S(1)} all-gather(bf16[128,1024]{1,0:T(8,128)(2,1)S(1)} %all_gather.6), channel_id=1, replica_groups=mesh['real'=2,'col'=8,'row'=2] {'row'}, dimensions={0}, use_global_device_ids=true | all-gather | bytes 786432 | tf_op jit(solution)/shard_map/all_gather | solution.py:42
  68.3 1.1 %fusion.1 = f32[1,1,16,256]{3,2,1,0:T(8,128)} fusion(bf16[256,1024]{1,0:T(8,128)(2,1)S(1)} %all_gather.7, bf16[1024,16]{1,0:T(8,128)(2,1)S(1)} %gather_fusion, pred[1024]{0:T(1024)(128)(4,1)S(1)} %compare_and_fusion), kind=kOutput, calls=%fused_computation.4 | convolution fusion | flops 8409088 | bytes 574464 | tf_op jit(solution)/shard_map/dot_general | solution.py:20
Async XLA Ops:
  2.6 21.7 %all-to-all-start = ((bf16[8,16,2048]{2,1,0:T(8,128)(2,1)}), bf16[8,16,2048]{2,1,0:T(8,128)(2,1)S(1)}, u32[]{:S(2)}, u32[]{:S(2)}) async-start(bf16[8,16,2048]{2,1,0:T(8,128)(2,1)} %bitcast.1), calls=%async_computation | async-start | bytes 1048576 | tf_op jit(solution)/shard_map/all_to_all | solution.py:37
where the time goes:
time: 69.8 us; the launch traced here: 69.4 us
  blocking collectives  32.9 us (47%)
  waiting for transfers between devices  13.1 us (19%)
  local copies, waits for them, and re-layouts  9.42 us (13%)
  starting transfers between devices  7.25 us (10%)
  other arithmetic  4.14 us (6%)
  matrix products  2.52 us (4%)
    all_gather x1, blocking collectives, per_device(): half_rows = lax.all_gather(sketch, 'col', axis=0, tiled=True)  30.7 us
    all_to_all x1, waiting for transfers between devices, per_device(): lax.all_to_all(scaled, 'col', split_axis=0, concat_axis=1, tiled=True)  13.1 us
    all_to_all x1, starting transfers between devices, per_device(): lax.all_to_all(scaled, 'col', split_axis=0, concat_axis=1, tiled=True)  7.25 us
    gather x1, local copies, waits for them, and re-layouts, per_device(): sketch = jnp.take(transformed, kept, axis=1).astype(jnp.bfloat16)  5.6 us
    div x1, local copies, waits for them, and re-layouts, per_device(): transformed = two_factor(spread) / SIDE  3.17 us
    all_gather x1, blocking collectives, per_device(): gram = against(sketch, lax.all_gather(half_rows, 'row', axis=0, tiled=True))  2.17 us
    mul x1, other arithmetic, per_device(): scaled = theta * signs.astype(jnp.bfloat16)[None, :]  1.86 us
  transfers between devices with their start and end apart: 1, of which 1 were waited for; matrix products, arithmetic and copies ran while one was open for 2% of the time, Pallas kernels for 0%

commit v1 on v0

v1 whole, which is shorter than its diff:
```python
import functools

import jax
import jax.numpy as jnp
from jax import lax
from jax.experimental import pallas as pl
from jax.experimental.pallas import tpu as pltpu
from jax.sharding import PartitionSpec as P

LANES = 128
PACKED = 16
BUDGET = 40 * 1024 * 1024
MESH = pl.DeviceIdType.MESH
CONTRACT_LAST = (((1,), (1,)), ((), ()))


def signs_of(bits, dtype):
    return (1 - 2 * (lax.population_count(bits) & 1)).astype(jnp.float32).astype(dtype)


def fill_walsh(target, columns, first):
    depth, width = target.shape
    within = lax.broadcasted_iota(jnp.int32, (LANES, width), 0) + first
    blocks = [signs_of(within & columns, jnp.bfloat16)]
    step = LANES
    while step < depth:
        flip = jnp.broadcast_to(signs_of(columns & step, jnp.float32), (LANES, width)).astype(jnp.bfloat16)
        blocks = blocks + [block * flip for block in blocks]
        step *= 2
    for place, block in enumerate(blocks):
        target[pl.ds(place * LANES, LANES), :] = block


def sketch_kernel(
    n_col, n_row, theta_ref, signs_ref, kept_ref, out_ref,
    theta, walsh, parts, got, both, products, arrived,
    load_sem, part_send, part_recv, row_send, row_recv, gram_send, gram_recv,
):
    col, row = lax.axis_index("col"), lax.axis_index("row")
    rows, depth = theta.shape
    width = parts.shape[2]
    own = out_ref.shape[0]

    barrier = pltpu.get_barrier_semaphore()
    for step in range(1, n_col):
        pl.semaphore_signal(barrier, inc=1, device_id={"col": lax.rem(col + step, n_col)}, device_id_type=MESH)
    for step in range(1, n_row):
        pl.semaphore_signal(barrier, inc=1, device_id={"row": lax.rem(row + step, n_row)}, device_id_type=MESH)
    load = pltpu.make_async_copy(theta_ref, theta, load_sem)
    load.start()

    order = sorted(range(n_col), key=lambda step: -min(step, n_col - step))
    groups = [order[place:place + 2] for place in range(0, n_col, 2)]

    def columns_of(group):
        pieces = []
        for step in group:
            owner = lax.rem(col + step, n_col)
            pieces.append(kept_ref[:, pl.ds(pl.multiple_of(owner * width, LANES), width)])
        return jnp.concatenate(pieces, axis=1)

    first = col * depth
    fill_walsh(walsh.at[0], columns_of(groups[0]), first)
    flips = jnp.broadcast_to(signs_ref[...].astype(jnp.float32), (PACKED, depth)).astype(jnp.bfloat16)
    load.wait()
    for place in range(0, rows, PACKED):
        theta[pl.ds(place, PACKED), :] = theta[pl.ds(place, PACKED), :] * flips

    sends = []
    mine = None
    for place, group in enumerate(groups):
        if place:
            fill_walsh(walsh.at[place], columns_of(group), first)
        part = jnp.dot(theta[...], walsh[place], preferred_element_type=jnp.float32)
        if place == 0:
            pl.semaphore_wait(barrier, n_col + n_row - 2)
        for index, step in enumerate(group):
            piece = part[:, index * width:(index + 1) * width]
            if step == 0:
                mine = piece
                continue
            parts[step] = piece.astype(jnp.bfloat16)
            copy = pltpu.make_async_remote_copy(
                src_ref=parts.at[step], dst_ref=got.at[step],
                send_sem=part_send.at[step], recv_sem=part_recv.at[step],
                device_id={"col": lax.rem(col + step, n_col)}, device_id_type=MESH,
            )
            copy.start()
            sends.append((step, copy))

    total = mine
    for step, copy in reversed(sends):
        copy.wait_recv()
        total = total + got[step].astype(jnp.float32)
    sketch = total.astype(jnp.bfloat16)
    both[row] = sketch
    row_copies = []
    for step in range(1, n_row):
        copy = pltpu.make_async_remote_copy(
            src_ref=both.at[row], dst_ref=both.at[row],
            send_sem=row_send.at[step], recv_sem=row_recv.at[step],
            device_id={"row": lax.rem(row + step, n_row)}, device_id_type=MESH,
        )
        copy.start()
        row_copies.append(copy)
    for copy in row_copies:
        copy.wait_recv()
    everything = both[...].reshape(n_row * rows, width)
    gram = lax.dot_general(sketch, everything, CONTRACT_LAST, preferred_element_type=jnp.float32)
    products[...] = gram.astype(jnp.bfloat16).reshape(products.shape)
    gram_copies = []
    for step in order:
        if step == 0:
            continue
        owner = lax.rem(col + step, n_col)
        copy = pltpu.make_async_remote_copy(
            src_ref=products.at[owner], dst_ref=arrived.at[step],
            send_sem=gram_send.at[step], recv_sem=gram_recv.at[step],
            device_id={"col": owner}, device_id_type=MESH,
        )
        copy.start()
        gram_copies.append((step, copy))
    total = products[col].astype(jnp.float32)
    for step, copy in reversed(gram_copies):
        copy.wait_recv()
        total = total + arrived[step].astype(jnp.float32)
    scale = 1.0 / (n_col * depth * kept_ref.shape[1])
    out_ref[...] = total * scale
    for _, copy in sends + gram_copies:
        copy.wait_send()
    for copy in row_copies:
        copy.wait_send()


def fused(n_col, n_row, theta, signs, kept):
    rows, depth = theta.shape
    keep = kept.shape[0]
    width = keep // n_col
    own = rows // n_col
    bf16 = jnp.bfloat16
    dma = pltpu.SemaphoreType.DMA
    vmem = pl.BlockSpec(memory_space=pltpu.VMEM)
    gram = pl.pallas_call(
        functools.partial(sketch_kernel, n_col, n_row),
        out_shape=jax.ShapeDtypeStruct((own, n_row * rows), jnp.float32),
        in_specs=[pl.BlockSpec(memory_space=pl.ANY), vmem, vmem],
        out_specs=vmem,
        scratch_shapes=[
            pltpu.VMEM((rows, depth), bf16),
            pltpu.VMEM((n_col // 2, depth, 2 * width), bf16),
            pltpu.VMEM((n_col, rows, width), bf16),
            pltpu.VMEM((n_col, rows, width), bf16),
            pltpu.VMEM((n_row, rows, width), bf16),
            pltpu.VMEM((n_col, own, n_row * rows), bf16),
            pltpu.VMEM((n_col, own, n_row * rows), bf16),
            dma,
            dma((n_col,)), dma((n_col,)),
            dma((n_row,)), dma((n_row,)),
            dma((n_col,)), dma((n_col,)),
        ],
        compiler_params=pltpu.CompilerParams(
            collective_id=0, has_side_effects=True, vmem_limit_bytes=BUDGET
        ),
        cost_estimate=pl.CostEstimate(
            flops=2 * rows * depth * keep, bytes_accessed=2 * rows * depth, transcendentals=0
        ),
    )(theta, signs[None, :], kept[None, :])
    return gram.reshape(1, 1, own, n_row * rows)


def hadamard(order, dtype):
    indices = jnp.arange(order, dtype=jnp.int32)
    return signs_of(indices[:, None] & indices[None, :], dtype)


def gathered(n_col, side, theta, signs, kept):
    scaled = theta * signs.astype(jnp.bfloat16)[None, :]
    spread = lax.all_to_all(scaled, "col", split_axis=0, concat_axis=1, tiled=True)
    height = spread.shape[0]
    inner = jnp.dot(
        spread.reshape(height * side, side), hadamard(side, jnp.bfloat16), preferred_element_type=jnp.float32
    ).reshape(height, side, side)
    outer = jnp.einsum("rak,aj->rjk", inner, hadamard(side, jnp.float32), precision=lax.Precision.HIGHEST)
    transformed = outer.reshape(height, side * side) / side
    sketch = jnp.take(transformed, kept, axis=1).astype(jnp.bfloat16)
    half_rows = lax.all_gather(sketch, "col", axis=0, tiled=True)
    every = lax.all_gather(half_rows, "row", axis=0, tiled=True)
    gram = lax.dot_general(sketch, every, CONTRACT_LAST, preferred_element_type=jnp.float32)
    return gram / kept.shape[0]


def solution(mesh):
    n_col, n_row = mesh.shape["col"], mesh.shape["row"]

    def per_device(theta, signs, kept):
        rows, depth = theta.shape
        keep = kept.shape[0]
        aligned = keep % (n_col * LANES) == 0 and rows % (n_col * PACKED) == 0 and depth % LANES == 0
        held = 2 * (rows * depth + depth * keep + 3 * rows * keep + 4 * rows * n_row * rows)
        if aligned and n_col % 2 == 0 and 2 * held <= BUDGET:
            return fused(n_col, n_row, theta, signs, kept)
        columns = depth * n_col
        side = 1 << (columns.bit_length() - 1) // 2
        gram = gathered(n_col, side, theta, signs, kept)
        return gram[None, None]

    return jax.shard_map(
        per_device,
        mesh=mesh,
        in_specs=(P(("real", "row"), "col"), P(("real", "col")), P()),
        out_specs=P(("real", "row"), "col", None, None),
        check_vma=False,
    )
```

time: 69.8 us -> 21.5 us (0.31)
  blocking collectives: 32.9 us -> 0 us
  Pallas kernels: 0 us -> 18.2 us
  waiting for transfers between devices: 13.1 us -> 0 us
  starting transfers between devices: 7.25 us -> 0 us
  local copies, waits for them, and re-layouts: 9.42 us -> 3.03 us
  other arithmetic: 4.14 us -> 0 us
  matrix products: 2.52 us -> 0 us
    all_gather x2 -> x0, blocking collectives: 32.9 us -> none  [the longest x1 30.7 us: per_device(): half_rows = lax.all_gather(sketch, 'col', axis=0, tiled=True)]
    pallas_call x0 -> x1, Pallas kernels: none -> 18.2 us  [fused(): pl.pallas_call(functools.partial(sketch_kernel, n_col, n_row), out_shape=...]
    all_to_all x1 -> x0, waiting for transfers between devices: 13.1 us -> none  [per_device(): lax.all_to_all(scaled, 'col', split_axis=0, concat_axis=1, tiled=True)]
    all_to_all x1 -> x0, starting transfers between devices: 7.25 us -> none  [per_device(): lax.all_to_all(scaled, 'col', split_axis=0, concat_axis=1, tiled=True)]
    gather x1 -> x0, local copies, waits for them, and re-layouts: 5.6 us -> none  [per_device(): sketch = jnp.take(transformed, kept, axis=1).astype(jnp.bfloat16)]
    div x1 -> x0, local copies, waits for them, and re-layouts: 3.17 us -> none  [per_device(): transformed = two_factor(spread) / SIDE]
    unnamed x0 -> x7, local copies, waits for them, and re-layouts: none -> 3.03 us
    dot_general x3 -> x0, matrix products: 2.52 us -> none  [the longest x1 1.11 us: against(): return jnp.dot(left, right.T, preferred_element_type=jnp.float32)]
  transfers between devices with their start and end apart: 1 -> 0, of which waited for: 1 -> 0; matrix products, arithmetic and copies ran while one was open for 2% -> 0% of each run, Pallas kernels for 0% -> 0%
where the time goes in v1:
time: 21.5 us; the launch traced here: 21.2 us
  Pallas kernels  18.2 us (85%)
  local copies, waits for them, and re-layouts  3.03 us (14%)
    pallas_call x1, Pallas kernels, fused(): pl.pallas_call(functools.partial(sketch_kernel, n_col, n_row), out_shape=...  18.2 us
    unnamed x7, local copies, waits for them, and re-layouts  3.03 us

profile of v1, /device:TPU:0, one launch (start us, length us, event | category | flops | bytes accessed | tf_op | source)
XLA Modules:
  0.0 21.2 jit_solution(11934903154590428899)
XLA Ops:
  0.0 0.0 copy-start
  0.0 1.0 %copy-done = bf16[128,2048]{1,0:T(8,128)(2,1)S(1)} copy-done((bf16[128,2048]{1,0:T(8,128)(2,1)S(1)}, bf16[128,2048]{1,0:T(8,128)(2,1)}, u32[]{:S(2)}) %copy-start) | copy-done | bytes 524312
  1.0 0.0 copy-start.1
  1.0 0.7 %copy-done.1 = s32[2048]{0:T(1024)S(1)} copy-done((s32[2048]{0:T(1024)S(1)}, s32[2048]{0:T(1024)}, u32[]{:S(2)}) %copy-start.1) | copy-done | bytes 8216
  1.7 0.0 copy-start.2
  1.7 0.7 %copy-done.2 = s32[1024]{0:T(1024)S(1)} copy-done((s32[1024]{0:T(1024)S(1)}, s32[1024]{0:T(1024)}, u32[]{:S(2)}) %copy-start.2) | copy-done | bytes 4120
  2.4 18.2 %shard_map.37 = f32[16,256]{1,0:T(8,128)S(1)} custom-call(bf16[128,2048]{1,0:T(8,128)(2,1)S(1)} %copy-done, s32[1,2048]{1,0:T(1,128)S(1)} %bitcast.4, s32[1,1024]{1,0:T(1,128)S(1)} %bitcast.5), custom_call_target="tpu_custom_call" | custom-call | flops 536870912 | bytes 524288 | tf_op jit(solution)/shard_map/pallas_call | solution.py:143
  20.6 0.6 %copy.5 = f32[1,1,16,256]{3,2,1,0:T(8,128)} copy(f32[1,1,16,256]{3,2,1,0:T(8,128)S(1)} %bitcast.3) | data formatting | bytes 32768
Async XLA Ops:
  0.0 1.0 %copy-start = (bf16[128,2048]{1,0:T(8,128)(2,1)S(1)}, bf16[128,2048]{1,0:T(8,128)(2,1)}, u32[]{:S(2)}) copy-start(bf16[128,2048]{1,0:T(8,128)(2,1)} %theta_ref.1) | copy-start | bytes 1572868
  1.0 0.7 %copy-start.1 = (s32[2048]{0:T(1024)S(1)}, s32[2048]{0:T(1024)}, u32[]{:S(2)}) copy-start(s32[2048]{0:T(1024)} %param.4) | copy-start | bytes 24580
  1.7 0.7 %copy-start.2 = (s32[1024]{0:T(1024)S(1)}, s32[1024]{0:T(1024)}, u32[]{:S(2)}) copy-start(s32[1024]{0:T(1024)} %param.5) | copy-start | bytes 12292

commit v2 on v1

--- a/solution.py
+++ b/solution.py
@@ -9,7 +9,7 @@
 
 LANES = 128
 PACKED = 16
-BUDGET = 40 * 1024 * 1024
+BUDGET = 60 * 1024 * 1024
 MESH = pl.DeviceIdType.MESH
 CONTRACT_LAST = (((1,), (1,)), ((), ()))
 
@@ -32,8 +32,8 @@
 
 
 def sketch_kernel(
-    n_col, n_row, theta_ref, signs_ref, kept_ref, out_ref,
-    theta, walsh, parts, got, both, products, arrived,
+    n_col, n_row, theta_in, signs_in, kept_in, out_ref,
+    theta, signs_ref, kept_ref, walsh, parts, got, both, products, arrived,
     load_sem, part_send, part_recv, row_send, row_recv, gram_send, gram_recv,
 ):
     col, row = lax.axis_index("col"), lax.axis_index("row")
@@ -46,8 +46,12 @@
         pl.semaphore_signal(barrier, inc=1, device_id={"col": lax.rem(col + step, n_col)}, device_id_type=MESH)
     for step in range(1, n_row):
         pl.semaphore_signal(barrier, inc=1, device_id={"row": lax.rem(row + step, n_row)}, device_id_type=MESH)
-    load = pltpu.make_async_copy(theta_ref, theta, load_sem)
-    load.start()
+    loads = [
+        pltpu.make_async_copy(source, target, load_sem.at[place])
+        for place, (source, target) in enumerate(((kept_in, kept_ref), (theta_in, theta), (signs_in, signs_ref)))
+    ]
+    for load in loads:
+        load.start()
 
     order = sorted(range(n_col), key=lambda step: -min(step, n_col - step))
     groups = [order[place:place + 2] for place in range(0, n_col, 2)]
@@ -60,9 +64,11 @@
         return jnp.concatenate(pieces, axis=1)
 
     first = col * depth
+    loads[0].wait()
     fill_walsh(walsh.at[0], columns_of(groups[0]), first)
+    loads[2].wait()
     flips = jnp.broadcast_to(signs_ref[...].astype(jnp.float32), (PACKED, depth)).astype(jnp.bfloat16)
-    load.wait()
+    loads[1].wait()
     for place in range(0, rows, PACKED):
         theta[pl.ds(place, PACKED), :] = theta[pl.ds(place, PACKED), :] * flips
 
@@ -143,17 +149,19 @@
     gram = pl.pallas_call(
         functools.partial(sketch_kernel, n_col, n_row),
         out_shape=jax.ShapeDtypeStruct((own, n_row * rows), jnp.float32),
-        in_specs=[pl.BlockSpec(memory_space=pl.ANY), vmem, vmem],
+        in_specs=[pl.BlockSpec(memory_space=pltpu.HBM)] * 3,
         out_specs=vmem,
         scratch_shapes=[
             pltpu.VMEM((rows, depth), bf16),
+            pltpu.VMEM((1, depth), jnp.int32),
+            pltpu.VMEM((1, keep), jnp.int32),
             pltpu.VMEM((n_col // 2, depth, 2 * width), bf16),
             pltpu.VMEM((n_col, rows, width), bf16),
             pltpu.VMEM((n_col, rows, width), bf16),
             pltpu.VMEM((n_row, rows, width), bf16),
             pltpu.VMEM((n_col, own, n_row * rows), bf16),
             pltpu.VMEM((n_col, own, n_row * rows), bf16),
-            dma,
+            dma((3,)),
             dma((n_col,)), dma((n_col,)),
             dma((n_row,)), dma((n_row,)),
             dma((n_col,)), dma((n_col,)),

time: 21.5 us -> 20.4 us (0.949)
  local copies, waits for them, and re-layouts: 3.03 us -> 1.32 us
  Pallas kernels: 18.2 us -> 18.8 us
    unnamed x7 -> x1, local copies, waits for them, and re-layouts: 3.03 us -> 1.32 us
    pallas_call x1, Pallas kernels: 18.2 us -> 18.8 us  [fused(): pl.pallas_call(functools.partial(sketch_kernel, n_col, n_row), out_shape=...]
where the time goes in v2:
time: 20.4 us; the launch traced here: 20.1 us
  Pallas kernels  18.8 us (92%)
  local copies, waits for them, and re-layouts  1.32 us (6%)
    pallas_call x1, Pallas kernels, fused(): pl.pallas_call(functools.partial(sketch_kernel, n_col, n_row), out_shape=...  18.8 us
    unnamed x1, local copies, waits for them, and re-layouts  1.32 us

profile of v2, /device:TPU:0, one launch (start us, length us, event | category | flops | bytes accessed | tf_op | source)
XLA Modules:
  0.0 20.1 jit_solution(18132199917085922274)
XLA Ops:
  0.0 18.8 %shard_map.37 = f32[16,256]{1,0:T(8,128)} custom-call(bf16[128,2048]{1,0:T(8,128)(2,1)} %theta_in.1, s32[1,2048]{1,0:T(1,128)} %bitcast.4, s32[1,1024]{1,0:T(1,128)} %bitcast.5), custom_call_target="tpu_custom_call" | custom-call | flops 536870912 | bytes 524288 | tf_op jit(solution)/shard_map/pallas_call | solution.py:149
  18.8 1.3 %copy.5 = f32[1,1,16,256]{3,2,1,0:T(8,128)} copy(f32[1,1,16,256]{3,2,1,0:T(8,128)} %bitcast.3) | data formatting | bytes 32768

commit v3 on v2

--- a/solution.py
+++ b/solution.py
@@ -9,7 +9,7 @@
 
 LANES = 128
 PACKED = 16
-BUDGET = 60 * 1024 * 1024
+BUDGET = 40 * 1024 * 1024
 MESH = pl.DeviceIdType.MESH
 CONTRACT_LAST = (((1,), (1,)), ((), ()))
 
@@ -172,7 +172,7 @@
         cost_estimate=pl.CostEstimate(
             flops=2 * rows * depth * keep, bytes_accessed=2 * rows * depth, transcendentals=0
         ),
-    )(theta, signs[None, :], kept[None, :])
+    )(*[pltpu.with_memory_space_constraint(each, pltpu.HBM) for each in (theta, signs[None, :], kept[None, :])])
     return gram.reshape(1, 1, own, n_row * rows)
 
 

time: 20.4 us -> 19 us (0.931)
  local copies, waits for them, and re-layouts: 1.32 us -> 0.61 us
  Pallas kernels: 18.8 us -> 18.2 us
    unnamed x1, local copies, waits for them, and re-layouts: 1.32 us -> 0.61 us
    pallas_call x1, Pallas kernels: 18.8 us -> 18.2 us  [fused(): pl.pallas_call(functools.partial(sketch_kernel, n_col, n_row), out_shape=...]
where the time goes in v3:
time: 19 us; the launch traced here: 18.8 us
  Pallas kernels  18.2 us (96%)
  local copies, waits for them, and re-layouts  0.61 us (3%)
    pallas_call x1, Pallas kernels, fused(): pl.pallas_call(functools.partial(sketch_kernel, n_col, n_row), out_shape=...  18.2 us
    unnamed x1, local copies, waits for them, and re-layouts  0.61 us

profile of v3, /device:TPU:0, one launch (start us, length us, event | category | flops | bytes accessed | tf_op | source)
XLA Modules:
  0.0 18.8 jit_solution(8889651924567519965)
XLA Ops:
  0.0 18.2 %shard_map.37 = f32[16,256]{1,0:T(8,128)S(1)} custom-call(bf16[128,2048]{1,0:T(8,128)(2,1)} %theta_in.1, s32[1,2048]{1,0:T(1,128)} %bitcast.4, s32[1,1024]{1,0:T(1,128)} %bitcast.5), custom_call_target="tpu_custom_call" | custom-call | flops 536870912 | bytes 524288 | tf_op jit(solution)/shard_map/pallas_call | solution.py:149
  18.2 0.6 %copy.5 = f32[1,1,16,256]{3,2,1,0:T(8,128)} copy(f32[1,1,16,256]{3,2,1,0:T(8,128)S(1)} %bitcast.3) | data formatting | bytes 32768
